TPU v7x, 512 devices: a whole 4x4x16 slice. The times are simulated.
512 devices in a mesh: row: 64 (over z, y), col: 8 (over x, core).
Axes of the slice: x: 4, y: 4, z: 16, core: 2. Of those that a mesh axis runs over, the one named last changes fastest.
Arguments:
- acts: bfloat16 [8192, 8192], P('row'), may hold values from -22 to 22
- out_grads: bfloat16 [8192, 4096], P('row', 'col'), may hold values from -0.099436891 to 0.099436891
- weight: float32 [8192, 4096], P('row', 'col'), may hold values from -30 to 30
- row_state: float32 [8192], P('row'), may hold values from 0.002 to 2
- col_state: float32 [4096], P('col'), may hold values from 0.01 to 0.3
Outputs:
- new_weight: float32 [8192, 4096], P('row', 'col')
- update: float32 [8192, 4096], P('row', 'col')
- row_moment: float32 [8192], P('row')
- col_moment: float32 [4096], P('col')
All inputs are finite; a program needn't handle non-finite values.
Results may differ from a plain program's by a relative error of at most 0.0003.
Values may be sent and summed in bfloat16 or wider, within the bound.
A program may use at most 64 MiB of HBM per device.

v0:
```python
import jax
import jax.numpy as jnp
from jax import lax
from jax.sharding import Mesh
from jax.sharding import PartitionSpec as P

Z, Y = ("row_0", "row_1")
ROW = (Z, Y)
COL = ("col_0", "col_1")
decay_rate = 0.85
floor_eps = 1e-30
relative_rate = 0.05


def per_device(acts, out_grads, weight, row_state, col_state):
    n_row = lax.axis_size(ROW)
    n_z = lax.axis_size(Z)
    n_y = lax.axis_size(Y)
    n_col = lax.axis_size(COL)
    tok_dev = acts.shape[0]
    width = acts.shape[1]
    cols_here = out_grads.shape[1]
    cols_all = cols_here * n_col
    share_rows = tok_dev // n_col
    own_rows = lax.dynamic_slice_in_dim(acts, lax.axis_index(COL) * share_rows, share_rows, 0)
    arrived = lax.all_to_all(own_rows, Z, split_axis=1, concat_axis=0, tiled=True)
    columns = lax.all_gather(
        arrived.reshape(n_z, share_rows, width // n_z), COL, axis=1, tiled=True
    )
    columns = columns.reshape(n_z * tok_dev, width // n_z)
    gathered = lax.all_gather(out_grads, Z, axis=0, tiled=True)
    partial = lax.dot_general(
        columns, gathered, (((0,), (0,)), ((), ())), preferred_element_type=jnp.float32
    )
    gradient = lax.psum_scatter(partial, Y, scatter_dimension=0, tiled=True)
    squares = gradient * gradient + floor_eps
    row_squares = jnp.sum(squares, axis=1)
    col_squares = jnp.sum(squares, axis=0)
    weight_part = jnp.sum(weight * weight)
    row_total = lax.psum(row_squares, COL)
    row_moment = decay_rate * row_state + (1.0 - decay_rate) * (row_total / cols_all)
    scaled = gradient * lax.rsqrt(row_moment)[:, None]
    stacked = jnp.concatenate([col_squares, jnp.sum(scaled * scaled, axis=0)])
    stacked = lax.psum(stacked, ROW)
    col_total, scaled_total = (stacked[:cols_here], stacked[cols_here:])
    col_moment = decay_rate * col_state + (1.0 - decay_rate) * (col_total / width)
    unclipped = gradient * lax.rsqrt(row_moment[:, None] * col_moment[None, :])
    update_total = lax.psum(jnp.sum(scaled_total / col_moment), COL)
    weight_total = lax.psum(weight_part, ROW + COL)
    count_all = width * cols_all
    clip_factor = jnp.maximum(1.0, jnp.sqrt(update_total / count_all))
    update = unclipped / clip_factor
    step_size = relative_rate * jnp.sqrt(weight_total / count_all + 1e-06)
    new_weight = weight - step_size * update
    return (new_weight, update, row_moment, col_moment)


def solution(mesh):
    finer = Mesh(mesh.devices.reshape(16, 4, 4, 2), (Z, Y) + COL)
    placed = (P(ROW, None), P(ROW, COL), P(ROW, COL), P(ROW), P(COL))
    return jax.shard_map(
        per_device,
        mesh=finer,
        in_specs=placed,
        out_specs=(P(ROW, COL), P(ROW, COL), P(ROW), P(COL)),
        check_vma=False,
    )
```

profile of v0, /device:TPU:1, one launch (start us, length us, event | category | flops | bytes accessed | tf_op | source)
XLA Modules:
  0.0 432.5 jit_solution(11988476071683671557)
XLA Ops:
  7.2 0.0 copy-start
  7.2 0.0 all-gather.3.cloned.1.call-start
  7.2 1.5 copy-done
  8.8 28.7 %all_to_all.16 = bf16[16,16,512]{2,0,1:T(8,128)(2,1)S(1)} all-to-all(bf16[16,16,512]{2,0,1:T(8,128)(2,1)S(1)} %bitcast.10), channel_id=1, replica_groups=mesh['row_0'=16,'row_1'=4,'col_0'=4,'col_1'=2] {'row_0'}, dimensions={1} | all-to-all | bytes 524288 | tf_op jit(solution)/shard_map/all_to_all | solution.py:26
  37.5 0.9 copy.11
  38.3 0.0 all-gather.3.cloned.1.call-update
  38.4 0.0 all-gather.5.cloned.1.call-start
  38.4 0.7 all-gather.5.cloned.1.call-update
  39.1 0.0 reduce-scatter.2.cloned.1.call-start
  39.2 33.2 %all-gather.3.cloned.1.call-done = bf16[16,128,512]{2,0,1:T(8,128)(2,1)} async-done(((bf16[16,16,512]{2,0,1:T(8,128)(2,1)}), bf16[16,128,512]{2,0,1:T(8,128)(2,1)}) %all-gather.3.cloned.1.call-update) | async-done | bytes 2097168 | tf_op jit(solution)/shard_map/all_gather | solution.py:27
  72.3 4.0 copy.12
  76.4 62.1 %all-gather.5.cloned.1.call-done = bf16[2048,512]{1,0:T(8,128)(2,1)} async-done(((bf16[128,512]{1,0:T(8,128)(2,1)}), bf16[2048,512]{1,0:T(8,128)(2,1)}) %all-gather.5.cloned.1.call-update) | async-done | bytes 2097168 | tf_op jit(solution)/shard_map/all_gather | solution.py:31
  138.5 0.0 copy-start.1
  138.5 0.0 copy-start.5
  138.5 0.0 copy-start.4
  138.5 4.5 %fusion.4 = f32[512,512]{1,0:T(8,128)} fusion(bf16[2048,512]{1,0:T(8,128)(2,1)} %bitcast.8, bf16[2048,512]{1,0:T(8,128)(2,1)} %all-gather.5.cloned.1.call-done), kind=kOutput, calls=%fused_computation.15 | convolution fusion | flops 1073741824 | bytes 5242880 | tf_op jit(solution)/shard_map/dot_general | solution.py:32
  143.0 0.0 reduce-scatter.2.cloned.1.call-update
  143.0 0.0 copy-done.1
  143.0 0.7 multiply_reduce_fusion.1
  143.7 110.9 %psum.28 = f32[]{:T(128)} all-reduce(f32[]{:T(128)} %multiply_reduce_fusion.1), channel_id=1, replica_groups=mesh['row_0'=16,'row_1'=4,'col_0'=4,'col_1'=2] {'row_0','row_1','col_0',..., use_global_device_ids=true, to_apply=%region_1.0 | all-reduce | flops 1 | bytes 8 | tf_op jit(solution)/shard_map/psum | solution.py:49
  255.2 0.0 reduce-scatter.2.cloned.1.call-done
  255.3 1.1 fusion.1
  256.3 12.4 %psum.29 = f32[128]{0:T(128)S(1)} all-reduce(f32[128]{0:T(128)S(1)} %fusion.1), channel_id=1, replica_groups=mesh['row_0'=16,'row_1'=4,'col_0'=4,'col_1'=2] {'col_0','col_1'}, use_global_device_ids=true, to_apply=%region_4.0 | all-reduce | flops 128 | bytes 1024 | tf_op jit(solution)/shard_map/psum | solution.py:40
  268.8 0.0 copy-done.5
  268.8 0.0 copy-start.3
  268.8 1.1 fusion
  269.9 112.1 %psum.30 = f32[1024]{0:T(1024)S(1)} all-reduce(f32[1024]{0:T(1024)S(1)} %pad_maximum_fusion), channel_id=1, replica_groups=mesh['row_0'=16,'row_1'=4,'col_0'=4,'col_1'=2] {'row_0','row_1'}, use_global_device_ids=true, to_apply=%region_7.0 | all-reduce | flops 1024 | bytes 8192 | tf_op jit(solution)/shard_map/psum | solution.py:44
  382.0 0.0 copy-done.4
  382.0 0.6 fusion.2
  382.6 0.0 copy-start.2
  382.6 40.8 %psum.31 = f32[]{:T(128)} all-reduce(f32[]{:T(128)} %get-tuple-element.8), channel_id=1, replica_groups=mesh['row_0'=16,'row_1'=4,'col_0'=4,'col_1'=2] {'col_0','col_1'}, use_global_device_ids=true, to_apply=%region_9.0 | all-reduce | flops 1 | bytes 8 | tf_op jit(solution)/shard_map/psum | solution.py:48
  424.1 1.9 multiply_subtract_fusion
  425.9 0.0 copy-done.3
  426.0 0.0 copy-done.2
  (4 shorter events, 0.1 us)
Async XLA Ops:
  7.2 1.6 copy-start
  7.2 65.1 %all-gather.3.cloned.1.call-start = ((), (), s32[]{:S(2)}) async-start(), calls=%async_computation.2 | async-start | bytes 2359296 | tf_op jit(solution)/shard_map/all_gather | solution.py:27
  38.4 100.1 %all-gather.5.cloned.1.call-start = ((), (), s32[]{:S(2)}) async-start(), calls=%async_computation.3 | async-start | bytes 2228224 | tf_op jit(solution)/shard_map/all_gather | solution.py:31
  39.1 216.1 %reduce-scatter.2.cloned.1.call-start = ((), (), s32[]{:S(2)}) async-start(), calls=%async_computation.4 | async-start | bytes 1310720 | tf_op jit(solution)/shard_map/reduce_scatter | solution.py:35
  138.5 4.5 %copy-start.1 = (f32[128,512]{1,0:T(8,128)S(1)}, f32[128,512]{1,0:T(8,128)}, u32[]{:S(2)}) copy-start(f32[128,512]{1,0:T(8,128)} %param.7) | copy-start | bytes 786436
  138.5 130.3 %copy-start.5 = (f32[128]{0:T(128)S(1)}, f32[128]{0:T(128)}, u32[]{:S(2)}) copy-start(f32[128]{0:T(128)} %param.8) | copy-start | bytes 1540
  138.5 243.5 %copy-start.4 = (f32[512]{0:T(512)S(1)}, f32[512]{0:T(512)}, u32[]{:S(2)}) copy-start(f32[512]{0:T(512)} %param.9) | copy-start | bytes 6148
  268.8 157.2 %copy-start.3 = (f32[128]{0:T(128)}, f32[128]{0:T(128)S(1)}, u32[]{:S(2)}) copy-start(f32[128]{0:T(128)S(1)} %get-tuple-element.11) | copy-start | bytes 1540
  382.6 43.4 %copy-start.2 = (f32[512]{0:T(512)}, f32[512]{0:T(512)S(1)}, u32[]{:S(2)}) copy-start(f32[512]{0:T(512)S(1)} %get-tuple-element.9) | copy-start | bytes 6148
Sparse Core Ops, SparseCore 0:
  38.5 33.7 all-gather.2
  74.4 64.0 all-gather.4
  143.1 36.4 reduce-scatter.1
where the time goes:
time: 433 us; the launch traced here: 432 us
  blocking collectives  305 us (70%)
  waiting for transfers between devices  96 us (22%)
  between operations  15.2 us (4%)
  local copies, waits for them, and re-layouts  6.49 us (1%)
  other arithmetic  5.28 us (1%)
  matrix products  4.51 us (1%)
    psum x1, blocking collectives, per_device(): stacked = lax.psum(stacked, ROW)  112 us
    psum x1, blocking collectives, per_device(): weight_total = lax.psum(weight_part, ROW + COL)  111 us
    all_gather x1, waiting for transfers between devices, per_device(): gathered = lax.all_gather(out_grads, Z, axis=0, tiled=True)  62.1 us
    psum x1, blocking collectives, per_device(): update_total = lax.psum(jnp.sum(scaled_total / col_moment), COL)  40.8 us
    all_gather x1, waiting for transfers between devices, per_device(): lax.all_gather(arrived.reshape(n_z, share_rows, width // n_z), COL, axis=...  33.2 us
    all_to_all x1, blocking collectives, per_device(): lax.all_to_all(own_rows, Z, split_axis=1, concat_axis=0, tiled=True)  28.7 us
    psum x1, blocking collectives, per_device(): row_total = lax.psum(row_squares, COL)  12.4 us
  transfers between devices with their start and end apart: 3, of which 2 were waited for; matrix products, arithmetic and copies ran while one was open for 1% of the time, Pallas kernels for 0%

commit v1 on v0

--- a/solution.py
+++ b/solution.py
@@ -41,7 +41,7 @@
     row_moment = decay_rate * row_state + (1.0 - decay_rate) * (row_total / cols_all)
     scaled = gradient * lax.rsqrt(row_moment)[:, None]
     stacked = jnp.concatenate([col_squares, jnp.sum(scaled * scaled, axis=0)])
-    stacked = lax.psum(stacked, ROW)
+    stacked = lax.psum(lax.psum(stacked, Y), Z)
     col_total, scaled_total = (stacked[:cols_here], stacked[cols_here:])
     col_moment = decay_rate * col_state + (1.0 - decay_rate) * (col_total / width)
     unclipped = gradient * lax.rsqrt(row_moment[:, None] * col_moment[None, :])

time: 433 us -> 330 us (0.76)
  blocking collectives: 305 us -> 202 us
    psum x1 -> x2, blocking collectives: 112 us -> 28.6 us  [per_device(): stacked = lax.psum(lax.psum(stacked, Y), Z)]
    psum x1, blocking collectives: 40.8 us -> 21.7 us  [per_device(): update_total = lax.psum(jnp.sum(scaled_total / col_moment), COL)]
where the time goes in v1:
time: 330 us
  blocking collectives  202 us (61%)
  waiting for transfers between devices  96 us (29%)
  between operations  15.2 us (5%)
  local copies, waits for them, and re-layouts  6.49 us (2%)
  other arithmetic  5.28 us (2%)
  matrix products  4.51 us (1%)
    psum x1, blocking collectives, per_device(): weight_total = lax.psum(weight_part, ROW + COL)  111 us
    all_gather x1, waiting for transfers between devices, per_device(): gathered = lax.all_gather(out_grads, Z, axis=0, tiled=True)  62.1 us
    all_gather x1, waiting for transfers between devices, per_device(): lax.all_gather(arrived.reshape(n_z, share_rows, width // n_z), COL, axis=...  33.2 us
    all_to_all x1, blocking collectives, per_device(): lax.all_to_all(own_rows, Z, split_axis=1, concat_axis=0, tiled=True)  28.7 us
    psum x2, blocking collectives, per_device(): stacked = lax.psum(lax.psum(stacked, Y), Z)  28.6 us
    psum x1, blocking collectives, per_device(): update_total = lax.psum(jnp.sum(scaled_total / col_moment), COL)  21.7 us
    psum x1, blocking collectives, per_device(): row_total = lax.psum(row_squares, COL)  12.4 us
  transfers between devices with their start and end apart: 3, of which 2 were waited for; matrix products, arithmetic and copies ran while one was open for 1% of the time, Pallas kernels for 0%

profile of v1, /device:TPU:1, one launch (start us, length us, event | category | flops | bytes accessed | tf_op | source)
XLA Modules:
  0.0 329.9 jit_solution(11088789163010058334)
XLA Ops:
  7.2 0.0 copy-start
  7.2 0.0 all-gather.3.cloned.1.call-start
  7.2 1.5 copy-done
  8.8 28.7 %all_to_all.16 = bf16[16,16,512]{2,0,1:T(8,128)(2,1)S(1)} all-to-all(bf16[16,16,512]{2,0,1:T(8,128)(2,1)S(1)} %bitcast.10), channel_id=1, replica_groups=mesh['row_0'=16,'row_1'=4,'col_0'=4,'col_1'=2] {'row_0'}, dimensions={1} | all-to-all | bytes 524288 | tf_op jit(solution)/shard_map/all_to_all | solution.py:26
  37.5 0.9 copy.11
  38.3 0.0 all-gather.3.cloned.1.call-update
  38.4 0.0 all-gather.5.cloned.1.call-start
  38.4 0.7 all-gather.5.cloned.1.call-update
  39.1 0.0 reduce-scatter.2.cloned.1.call-start
  39.2 33.2 %all-gather.3.cloned.1.call-done = bf16[16,128,512]{2,0,1:T(8,128)(2,1)} async-done(((bf16[16,16,512]{2,0,1:T(8,128)(2,1)}), bf16[16,128,512]{2,0,1:T(8,128)(2,1)}) %all-gather.3.cloned.1.call-update) | async-done | bytes 2097168 | tf_op jit(solution)/shard_map/all_gather | solution.py:27
  72.3 4.0 %copy.12 = bf16[16,128,512]{2,1,0:T(8,128)(2,1)} copy(bf16[16,128,512]{2,0,1:T(8,128)(2,1)} %all-gather.3.cloned.1.call-done) | data formatting | bytes 4194304 | tf_op jit(solution)/shard_map/all_gather | solution.py:27
  76.4 62.1 %all-gather.5.cloned.1.call-done = bf16[2048,512]{1,0:T(8,128)(2,1)} async-done(((bf16[128,512]{1,0:T(8,128)(2,1)}), bf16[2048,512]{1,0:T(8,128)(2,1)}) %all-gather.5.cloned.1.call-update) | async-done | bytes 2097168 | tf_op jit(solution)/shard_map/all_gather | solution.py:31
  138.5 0.0 copy-start.1
  138.5 0.0 copy-start.5
  138.5 0.0 copy-start.4
  138.5 4.5 %fusion.4 = f32[512,512]{1,0:T(8,128)} fusion(bf16[2048,512]{1,0:T(8,128)(2,1)} %bitcast.8, bf16[2048,512]{1,0:T(8,128)(2,1)} %all-gather.5.cloned.1.call-done), kind=kOutput, calls=%fused_computation.15 | convolution fusion | flops 1073741824 | bytes 5242880 | tf_op jit(solution)/shard_map/dot_general | solution.py:32
  143.0 0.0 reduce-scatter.2.cloned.1.call-update
  143.0 0.0 copy-done.1
  143.0 0.7 multiply_reduce_fusion.1
  143.7 110.9 %psum.35 = f32[]{:T(128)} all-reduce(f32[]{:T(128)} %multiply_reduce_fusion.1), channel_id=1, replica_groups=mesh['row_0'=16,'row_1'=4,'col_0'=4,'col_1'=2] {'row_0','row_1','col_0',..., use_global_device_ids=true, to_apply=%region_1.0 | all-reduce | flops 1 | bytes 8 | tf_op jit(solution)/shard_map/psum | solution.py:49
  255.2 0.0 reduce-scatter.2.cloned.1.call-done
  255.3 1.1 fusion.1
  256.3 12.4 %psum.36 = f32[128]{0:T(128)S(1)} all-reduce(f32[128]{0:T(128)S(1)} %fusion.1), channel_id=1, replica_groups=mesh['row_0'=16,'row_1'=4,'col_0'=4,'col_1'=2] {'col_0','col_1'}, use_global_device_ids=true, to_apply=%region_4.0 | all-reduce | flops 128 | bytes 1024 | tf_op jit(solution)/shard_map/psum | solution.py:40
  268.8 0.0 copy-done.5
  268.8 0.0 copy-start.3
  268.8 1.1 fusion
  269.9 8.3 %psum.37 = f32[1024]{0:T(1024)S(1)} all-reduce(f32[1024]{0:T(1024)S(1)} %pad_maximum_fusion), channel_id=1, replica_groups=mesh['row_0'=16,'row_1'=4,'col_0'=4,'col_1'=2] {'row_1'}, use_global_device_ids=true, to_apply=%region_7.0 | all-reduce | flops 1024 | bytes 8192 | tf_op jit(solution)/shard_map/psum | solution.py:44
  278.1 20.3 %psum.38 = f32[1024]{0:T(1024)S(1)} all-reduce(f32[1024]{0:T(1024)S(1)} %psum.37), channel_id=1, replica_groups=mesh['row_0'=16,'row_1'=4,'col_0'=4,'col_1'=2] {'row_0'}, use_global_device_ids=true, to_apply=%region_8.0 | all-reduce | flops 1024 | bytes 8192 | tf_op jit(solution)/shard_map/psum | solution.py:44
  298.4 0.0 copy-done.4
  298.4 0.6 fusion.2
  299.0 0.0 copy-start.2
  299.0 21.7 %psum.39 = f32[]{:T(128)} all-reduce(f32[]{:T(128)} %get-tuple-element.8), channel_id=1, replica_groups=mesh['row_0'=16,'row_1'=4,'col_0'=4,'col_1'=2] {'col_0','col_1'}, use_global_device_ids=true, to_apply=%region_10.0 | all-reduce | flops 1 | bytes 8 | tf_op jit(solution)/shard_map/psum | solution.py:48
  321.5 1.9 multiply_subtract_fusion
  323.3 0.0 copy-done.3
  323.3 0.0 copy-done.2
  (4 shorter events, 0.1 us)
Async XLA Ops:
  7.2 1.6 copy-start
  7.2 65.1 %all-gather.3.cloned.1.call-start = ((), (), s32[]{:S(2)}) async-start(), calls=%async_computation.2 | async-start | bytes 2359296 | tf_op jit(solution)/shard_map/all_gather | solution.py:27
  38.4 100.1 %all-gather.5.cloned.1.call-start = ((), (), s32[]{:S(2)}) async-start(), calls=%async_computation.3 | async-start | bytes 2228224 | tf_op jit(solution)/shard_map/all_gather | solution.py:31
  39.1 216.1 %reduce-scatter.2.cloned.1.call-start = ((), (), s32[]{:S(2)}) async-start(), calls=%async_computation.4 | async-start | bytes 1310720 | tf_op jit(solution)/shard_map/reduce_scatter | solution.py:35
  138.5 4.5 %copy-start.1 = (f32[128,512]{1,0:T(8,128)S(1)}, f32[128,512]{1,0:T(8,128)}, u32[]{:S(2)}) copy-start(f32[128,512]{1,0:T(8,128)} %param.7) | copy-start | bytes 786436
  138.5 130.3 %copy-start.5 = (f32[128]{0:T(128)S(1)}, f32[128]{0:T(128)}, u32[]{:S(2)}) copy-start(f32[128]{0:T(128)} %param.8) | copy-start | bytes 1540
  138.5 160.0 %copy-start.4 = (f32[512]{0:T(512)S(1)}, f32[512]{0:T(512)}, u32[]{:S(2)}) copy-start(f32[512]{0:T(512)} %param.9) | copy-start | bytes 6148
  268.8 54.6 %copy-start.3 = (f32[128]{0:T(128)}, f32[128]{0:T(128)S(1)}, u32[]{:S(2)}) copy-start(f32[128]{0:T(128)S(1)} %get-tuple-element.11) | copy-start | bytes 1540
  299.0 24.3 %copy-start.2 = (f32[512]{0:T(512)}, f32[512]{0:T(512)S(1)}, u32[]{:S(2)}) copy-start(f32[512]{0:T(512)S(1)} %get-tuple-element.9) | copy-start | bytes 6148
Sparse Core Ops, SparseCore 0:
  38.5 33.7 all-gather.2
  74.4 64.0 all-gather.4
  143.1 36.4 reduce-scatter.1

commit v2 on v0

--- a/solution.py
+++ b/solution.py
@@ -23,7 +23,9 @@
     cols_all = cols_here * n_col
     share_rows = tok_dev // n_col
     own_rows = lax.dynamic_slice_in_dim(acts, lax.axis_index(COL) * share_rows, share_rows, 0)
-    arrived = lax.all_to_all(own_rows, Z, split_axis=1, concat_axis=0, tiled=True)
+    arrived = jnp.concatenate(
+        lax.all_to_all(jnp.stack(jnp.split(own_rows, lax.axis_size(Z), axis=1)), Z, 0, 0), axis=0
+    )
     columns = lax.all_gather(
         arrived.reshape(n_z, share_rows, width // n_z), COL, axis=1, tiled=True
     )

time: 433 us -> 417 us (0.963)
  waiting for transfers between devices: 96 us -> 74.4 us
  local copies, waits for them, and re-layouts: 6.49 us -> 11.5 us
    all_gather x1, waiting for transfers between devices: 62.1 us -> 34.5 us  [per_device(): gathered = lax.all_gather(out_grads, Z, axis=0, tiled=True)]
    unnamed x12 -> x25, local copies, waits for them, and re-layouts: 1.56 us -> 10.8 us
    all_gather x1, waiting for transfers between devices: 33.2 us -> 39.2 us  [per_device(): lax.all_gather(arrived.reshape(n_z, share_rows, width // n_z), COL, axis=...]
    psum x1, blocking collectives: 111 us -> 105 us  [per_device(): weight_total = lax.psum(weight_part, ROW + COL)]
    all_to_all x1, blocking collectives: 28.7 us -> 34.2 us  [per_device(): lax.all_to_all(jnp.stack(jnp.split(own_rows, lax.axis_size(Z), axis=1)),...]
  transfers between devices with their start and end apart: 3 -> 3, of which waited for: 2 -> 2; matrix products, arithmetic and copies ran while one was open for 1% -> 3% of each run, Pallas kernels for 0% -> 0%
where the time goes in v2:
time: 417 us; the launch traced here: 416 us
  blocking collectives  305 us (73%)
  waiting for transfers between devices  74.4 us (18%)
  between operations  15.2 us (4%)
  local copies, waits for them, and re-layouts  11.5 us (3%)
  other arithmetic  5.28 us (1%)
  matrix products  4.51 us (1%)
    psum x1, blocking collectives, per_device(): stacked = lax.psum(stacked, ROW)  113 us
    psum x1, blocking collectives, per_device(): weight_total = lax.psum(weight_part, ROW + COL)  105 us
    psum x1, blocking collectives, per_device(): update_total = lax.psum(jnp.sum(scaled_total / col_moment), COL)  40.6 us
    all_gather x1, waiting for transfers between devices, per_device(): lax.all_gather(arrived.reshape(n_z, share_rows, width // n_z), COL, axis=...  39.2 us
    all_gather x1, waiting for transfers between devices, per_device(): gathered = lax.all_gather(out_grads, Z, axis=0, tiled=True)  34.5 us
    all_to_all x1, blocking collectives, per_device(): lax.all_to_all(jnp.stack(jnp.split(own_rows, lax.axis_size(Z), axis=1)),...  34.2 us
    psum x1, blocking collectives, per_device(): row_total = lax.psum(row_squares, COL)  12.4 us
    unnamed x25, local copies, waits for them, and re-layouts  10.8 us
  transfers between devices with their start and end apart: 3, of which 2 were waited for; matrix products, arithmetic and copies ran while one was open for 3% of the time, Pallas kernels for 0%

profile of v2, /device:TPU:1, one launch (start us, length us, event | category | flops | bytes accessed | tf_op | source)
XLA Modules:
  0.0 415.9 jit_solution(7228155236273388175)
XLA Ops:
  7.2 0.0 all-gather.5.cloned.1.call-start
  7.2 0.7 all-gather.5.cloned.1.call-update
  7.9 0.0 all-gather.3.cloned.1.call-start
  8.0 0.7 constant_dynamic-update-slice_fusion.15
  8.7 0.7 constant_dynamic-update-slice_fusion.14
  9.4 0.7 constant_dynamic-update-slice_fusion.13
  10.1 0.7 constant_dynamic-update-slice_fusion.12
  10.8 0.7 constant_dynamic-update-slice_fusion.11
  11.6 0.7 constant_dynamic-update-slice_fusion.10
  12.3 0.7 constant_dynamic-update-slice_fusion.9
  13.0 0.7 constant_dynamic-update-slice_fusion.8
  13.7 0.7 constant_dynamic-update-slice_fusion.7
  14.4 0.7 constant_dynamic-update-slice_fusion.6
  15.2 0.7 constant_dynamic-update-slice_fusion.5
  15.9 0.7 constant_dynamic-update-slice_fusion.4
  16.6 0.7 constant_dynamic-update-slice_fusion.3
  17.3 0.7 constant_dynamic-update-slice_fusion.2
  18.0 0.7 constant_dynamic-update-slice_fusion.1
  18.7 0.7 constant_dynamic-update-slice_fusion
  19.5 34.2 %all_to_all.5 = bf16[16,16,512]{2,1,0:T(8,128)(2,1)} all-to-all(bf16[16,16,512]{2,1,0:T(8,128)(2,1)S(1)} %constant_dynamic-update-slice_fusion), channel_id=1, replica_groups=mesh['row_0'=16,'row_1'=4,'col_0'=4,'col_1'=2] {'row_0'}, dimensions={0} | all-to-all | bytes 524288 | tf_op jit(solution)/shard_map/all_to_all | solution.py:27
  53.6 0.0 all-gather.3.cloned.1.call-update
  53.6 0.0 reduce-scatter.2.cloned.1.call-start
  53.7 34.5 %all-gather.5.cloned.1.call-done = bf16[2048,512]{1,0:T(8,128)(2,1)} async-done(((bf16[128,512]{1,0:T(8,128)(2,1)}), bf16[2048,512]{1,0:T(8,128)(2,1)}) %all-gather.5.cloned.1.call-update) | async-done | bytes 2097168 | tf_op jit(solution)/shard_map/all_gather | solution.py:33
  88.2 39.2 %all-gather.3.cloned.1.call-done = bf16[16,128,512]{2,1,0:T(8,128)(2,1)} async-done(((bf16[16,16,512]{2,1,0:T(8,128)(2,1)}), bf16[16,128,512]{2,1,0:T(8,128)(2,1)}) %all-gather.3.cloned.1.call-update) | async-done | bytes 2097168 | tf_op jit(solution)/shard_map/all_gather | solution.py:29
  127.4 0.0 copy-start
  127.4 0.0 copy-start.4
  127.4 0.0 copy-start.3
  127.4 4.5 %fusion.4 = f32[512,512]{1,0:T(8,128)} fusion(bf16[2048,512]{1,0:T(8,128)(2,1)} %bitcast.67, bf16[2048,512]{1,0:T(8,128)(2,1)} %all-gather.5.cloned.1.call-done), kind=kOutput, calls=%fused_computation.45 | convolution fusion | flops 1073741824 | bytes 5242880 | tf_op jit(solution)/shard_map/dot_general | solution.py:34
  131.9 0.0 reduce-scatter.2.cloned.1.call-update
  132.0 0.0 copy-done
  132.0 0.7 multiply_reduce_fusion.1
  132.6 104.9 %psum.28 = f32[]{:T(128)} all-reduce(f32[]{:T(128)} %multiply_reduce_fusion.1), channel_id=1, replica_groups=mesh['row_0'=16,'row_1'=4,'col_0'=4,'col_1'=2] {'row_0','row_1','col_0',..., use_global_device_ids=true, to_apply=%region_1.0 | all-reduce | flops 1 | bytes 8 | tf_op jit(solution)/shard_map/psum | solution.py:51
  238.2 0.0 reduce-scatter.2.cloned.1.call-done
  238.3 1.1 fusion.1
  239.3 12.4 %psum.29 = f32[128]{0:T(128)S(1)} all-reduce(f32[128]{0:T(128)S(1)} %fusion.1), channel_id=1, replica_groups=mesh['row_0'=16,'row_1'=4,'col_0'=4,'col_1'=2] {'col_0','col_1'}, use_global_device_ids=true, to_apply=%region_4.0 | all-reduce | flops 128 | bytes 1024 | tf_op jit(solution)/shard_map/psum | solution.py:42
  251.8 0.0 copy-done.4
  251.8 0.0 copy-start.2
  251.8 1.1 fusion
  252.9 112.7 %psum.30 = f32[1024]{0:T(1024)S(1)} all-reduce(f32[1024]{0:T(1024)S(1)} %pad_maximum_fusion), channel_id=1, replica_groups=mesh['row_0'=16,'row_1'=4,'col_0'=4,'col_1'=2] {'row_0','row_1'}, use_global_device_ids=true, to_apply=%region_7.0 | all-reduce | flops 1024 | bytes 8192 | tf_op jit(solution)/shard_map/psum | solution.py:46
  365.5 0.0 copy-done.3
  365.5 0.6 fusion.2
  366.2 0.0 copy-start.1
  366.2 40.6 %psum.31 = f32[]{:T(128)} all-reduce(f32[]{:T(128)} %get-tuple-element.8), channel_id=1, replica_groups=mesh['row_0'=16,'row_1'=4,'col_0'=4,'col_1'=2] {'col_0','col_1'}, use_global_device_ids=true, to_apply=%region_9.0 | all-reduce | flops 1 | bytes 8 | tf_op jit(solution)/shard_map/psum | solution.py:50
  407.5 1.9 multiply_subtract_fusion
  409.4 0.0 copy-done.2
  409.4 0.0 copy-done.1
  (2 shorter events, 0.0 us)
Async XLA Ops:
  7.2 81.0 %all-gather.5.cloned.1.call-start = ((), (), s32[]{:S(2)}) async-start(), calls=%async_computation.3 | async-start | bytes 2228224 | tf_op jit(solution)/shard_map/all_gather | solution.py:33
  7.9 119.5 %all-gather.3.cloned.1.call-start = ((), (), s32[]{:S(2)}) async-start(), calls=%async_computation.2 | async-start | bytes 2359296 | tf_op jit(solution)/shard_map/all_gather | solution.py:29
  53.6 184.6 %reduce-scatter.2.cloned.1.call-start = ((), (), s32[]{:S(2)}) async-start(), calls=%async_computation.4 | async-start | bytes 1310720 | tf_op jit(solution)/shard_map/reduce_scatter | solution.py:37
  127.4 4.5 %copy-start = (f32[128,512]{1,0:T(8,128)S(1)}, f32[128,512]{1,0:T(8,128)}, u32[]{:S(2)}) copy-start(f32[128,512]{1,0:T(8,128)} %param.7) | copy-start | bytes 786436
  127.4 124.4 %copy-start.4 = (f32[128]{0:T(128)S(1)}, f32[128]{0:T(128)}, u32[]{:S(2)}) copy-start(f32[128]{0:T(128)} %param.8) | copy-start | bytes 1540
  127.4 238.1 %copy-start.3 = (f32[512]{0:T(512)S(1)}, f32[512]{0:T(512)}, u32[]{:S(2)}) copy-start(f32[512]{0:T(512)} %param.9) | copy-start | bytes 6148
  251.8 157.6 %copy-start.2 = (f32[128]{0:T(128)}, f32[128]{0:T(128)S(1)}, u32[]{:S(2)}) copy-start(f32[128]{0:T(128)S(1)} %get-tuple-element.11) | copy-start | bytes 1540
  366.2 43.2 %copy-start.1 = (f32[512]{0:T(512)}, f32[512]{0:T(512)S(1)}, u32[]{:S(2)}) copy-start(f32[512]{0:T(512)S(1)} %get-tuple-element.9) | copy-start | bytes 6148
Sparse Core Ops, SparseCore 0:
  10.1 78.0 all-gather.4
  90.3 37.0 all-gather.2
  132.1 29.2 reduce-scatter.1
